TPU v7x, 1024 devices: a whole 8x8x8 slice. The times are simulated.
1024 devices in a mesh: row: 16 (over z, y_hi), col: 64 (over x, y_lo, core).
Axes of the slice: x: 8, y: 8 (y_hi: 2, y_lo: 4; y = y_hi * 4 + y_lo), z: 8, core: 2. Of those that a mesh axis runs over, the one named last changes fastest.
Arguments:
- vectors: float32 [1536, 384, 128], P('row', 'col'), may hold values from -0.02734375 to 0.02734375
- hblocks: float32 [384, 7, 128, 128], P('col'), may hold values from -1 to 1, as said below
- coupling: int32 [384, 6], P('col'), may hold values from 0 to 1, as said below
Outputs:
- projected_ham: float32 [1536, 1536], P('row', 'col')
- intersection: float32 [1536, 1536], P('row', 'col')
Inputs may be any that keep to these rules, and one draw needn't show every extreme that they name: For 1 <= k <= 3 and a >= k, hblocks[a, 3 - k] is the transpose of hblocks[a - k, 3 + k], and hblocks[a, 3] is symmetric, so the Hamiltonian is symmetric. coupling[a, 3 + k - 1] equals coupling[a + k, 3 - k] for 1 <= k <= 3; entries that name an atom outside the chain are 0.
All inputs are finite; a program needn't handle non-finite values.
Results may differ from a plain program's by a relative error of at most 0.0001.
Values sent between devices are 32-bit elements; how exact they have to be, the bound alone decides.
A program may use at most 64 MiB of HBM per device.

v0:
```python
import jax
import jax.numpy as jnp
from jax import lax
from jax.sharding import PartitionSpec as P

REACH = 3
DEGREE = 3


CENTER = 0.5
HALF_WIDTH = 1.5
HSCALE = 0.1


def with_halo(block, sides, width):
    for axis, dim in sides:
        count = lax.axis_size(axis)
        forward = [(i, i + 1) for i in range(count - 1)]
        backward = [(target, source) for source, target in forward]
        low = lax.ppermute(
            lax.slice_in_dim(block, block.shape[dim] - width, None, axis=dim), axis, forward
        )
        high = lax.ppermute(lax.slice_in_dim(block, 0, width, axis=dim), axis, backward)
        block = jnp.concatenate([low, block, high], axis=dim)
    return block


def masked_blocks(hblocks, coupling):
    ones = jnp.ones((coupling.shape[0], 1), jnp.int32)
    presence = jnp.concatenate([coupling[:, :REACH], ones, coupling[:, REACH:]], axis=1)
    return HSCALE * hblocks * presence.astype(jnp.float32)[:, :, None, None]


def apply_ham(field, blocks):
    atoms = field.shape[1]
    padded = with_halo(field, (("col", 1),), REACH)
    stacked = jnp.stack(
        [padded[:, offset : offset + atoms, :] for offset in range(2 * REACH + 1)], axis=2
    )
    return jnp.einsum("sakj,akij->sai", stacked, blocks, precision=lax.Precision.HIGHEST)


def block_product(left, piece):
    flat_piece = piece.reshape(piece.shape[0], -1)
    return jnp.einsum("sn,tn->st", left, flat_piece, precision=lax.Precision.HIGHEST)


def per_device(vectors, hblocks, coupling):
    blocks = masked_blocks(hblocks, coupling)
    y_prev = vectors
    y_now = (apply_ham(vectors, blocks) - CENTER * vectors) / HALF_WIDTH
    for section in range(DEGREE - 1):
        y_next = 2.0 * (apply_ham(y_now, blocks) - CENTER * y_now) / HALF_WIDTH - y_prev
        y_prev = y_now
        y_now = y_next
    own_rows = y_now.reshape(y_now.shape[0], -1)
    image = apply_ham(y_now, blocks)
    first = block_product(own_rows, lax.all_gather(image, "row", axis=0, tiled=True))
    second = block_product(own_rows, lax.all_gather(y_now, "row", axis=0, tiled=True))
    projected_ham, intersection = (
        lax.psum_scatter(first, "col", scatter_dimension=1, tiled=True),
        lax.psum_scatter(second, "col", scatter_dimension=1, tiled=True),
    )
    return (projected_ham, intersection)


def solution(mesh):
    in_specs = (P("row", "col", None), P("col", None, None, None), P("col", None))
    out_specs = (P("row", "col"), P("row", "col"))
    return jax.shard_map(
        per_device, mesh=mesh, in_specs=in_specs, out_specs=out_specs, check_vma=False
    )
```

profile of v0, /device:TPU:119, one launch (start us, length us, event | category | flops | bytes accessed | tf_op | source)
XLA Modules:
  0.0 934.9 jit_solution(9335789075315584717)
XLA Ops:
  7.2 1.0 fusion.124
  8.3 2.6 collective-permute-start.1
  10.8 6.9 collective-permute-start
  17.7 0.8 fusion.125
  18.6 0.1 pad.13.clone
  18.7 0.1 fusion.120
  18.7 1.1 collective-permute-done
  19.8 1.0 constant_dynamic-update-slice_fusion.3
  21.1 1.5 copy-done
  22.7 3.5 broadcast_multiply_fusion
  26.2 8.3 collective-permute-start.2
  34.5 1.9 collective-permute-start.3
  36.4 0.2 collective-permute-done.2
  36.7 8.2 collective-permute-done.3
  45.0 3.5 fusion.61
  48.6 1.9 collective-permute-start.4
  50.5 2.4 collective-permute-start.5
  53.0 8.0 collective-permute-done.5
  61.1 4.2 fusion.46
  65.4 1.0 fusion.121
  66.5 1.9 collective-permute-start.6
  68.4 2.6 collective-permute-start.7
  71.0 0.9 fusion.77
  71.9 0.9 fusion.74
  72.9 5.8 collective-permute-done.7
  78.8 4.2 fusion.28
  83.1 121.2 %all-gather.5.cloned.1.call-done = f32[1536,6,128]{2,0,1:T(8,128)} async-done(((f32[96,6,128]{2,0,1:T(8,128)}), f32[1536,6,128]{2,0,1:T(8,128)}) %all-gather.5.cloned.1.call-update) | async-done | bytes 4718608 | tf_op jit(solution)/shard_map/all_gather | solution.py:59
  204.4 7.1 convolution_bitcast_fusion
  211.5 137.8 %all-gather.3.cloned.1.call-done = f32[1536,6,128]{2,0,1:T(8,128)} async-done(((f32[96,6,128]{2,0,1:T(8,128)}), f32[1536,6,128]{2,0,1:T(8,128)}) %all-gather.3.cloned.1.call-update) | async-done | bytes 4718608 | tf_op jit(solution)/shard_map/all_gather | solution.py:58
  349.3 7.1 convolution_bitcast_fusion.1
  356.5 287.3 %reduce-scatter.11.cloned.1.call-done = f32[96,24]{0,1:T(8,128)} async-done(((f32[96,1536]{0,1:T(8,128)}), f32[96,24]{0,1:T(8,128)}) %reduce-scatter.11.cloned.1.call-update) | async-done | bytes 9232
  643.8 284.6 %reduce-scatter.9.cloned.1.call-done = f32[96,24]{0,1:T(8,128)} async-done(((f32[96,1536]{0,1:T(8,128)}), f32[96,24]{0,1:T(8,128)}) %reduce-scatter.9.cloned.1.call-update) | async-done | bytes 9232
  (46 shorter events, 0.9 us)
Async XLA Ops:
  7.2 13.8 %copy-start.2 = (f32[96,6,128]{2,0,1:T(8,128)S(1)}, f32[96,6,128]{2,0,1:T(8,128)}, u32[]{:S(2)}) copy-start(f32[96,6,128]{2,0,1:T(8,128)} %param.3) | copy-start | bytes 884740
  7.2 197.2 %all-gather.5.cloned.1.call-start = ((), (), s32[]{:S(2)}) async-start(), calls=%async_computation.3 | async-start | bytes 5013504 | tf_op jit(solution)/shard_map/all_gather | solution.py:59
  8.3 12.7 %collective-permute-start.1 = (f32[96,3,128]{2,0,1:T(8,128)S(1)}, f32[96,3,128]{2,0,1:T(8,128)S(1)}, u32[]{:S(2)}, u32[]{:S(2)}) collective-permute-start(f32[96,3,128]{2,0,1:T(8,128)S(1)} %get-tuple-element.8), channel_id=1, source_target_pairs={{1,0},{2,1},{3,2},{4,3},{5,4},{6,5},{7,6},{8,7},{9,8},{10,9},{11,1... | collective-permute-start | bytes 442376 | tf_op jit(solution)/shard_map/ppermute | solution.py:23
  10.8 9.0 collective-permute-start
  20.9 1.8 copy-start
  26.2 10.4 %collective-permute-start.2 = (f32[96,3,128]{2,0,1:T(8,128)S(1)}, f32[96,3,128]{2,0,1:T(8,128)S(1)}, u32[]{:S(2)}, u32[]{:S(2)}) collective-permute-start(f32[96,3,128]{2,0,1:T(8,128)S(1)} %get-tuple-element.7), channel_id=1, source_target_pairs={{0,1},{1,2},{2,3},{3,4},{4,5},{5,6},{6,7},{7,8},{8,9},{9,10},{10,1... | collective-permute-start | bytes 442376 | tf_op jit(solution)/shard_map/ppermute | solution.py:20
  34.5 10.4 %collective-permute-start.3 = (f32[96,3,128]{2,0,1:T(8,128)S(1)}, f32[96,3,128]{2,0,1:T(8,128)S(1)}, u32[]{:S(2)}, u32[]{:S(2)}) collective-permute-start(f32[96,3,128]{2,0,1:T(8,128)S(1)} %get-tuple-element.6), channel_id=1, source_target_pairs={{1,0},{2,1},{3,2},{4,3},{5,4},{6,5},{7,6},{8,7},{9,8},{10,9},{11,1... | collective-permute-start | bytes 442376 | tf_op jit(solution)/shard_map/ppermute | solution.py:23
  48.6 4.3 collective-permute-start.4
  50.5 10.5 %collective-permute-start.5 = (f32[96,3,128]{2,0,1:T(8,128)S(1)}, f32[96,3,128]{2,0,1:T(8,128)S(1)}, u32[]{:S(2)}, u32[]{:S(2)}) collective-permute-start(f32[96,3,128]{2,0,1:T(8,128)S(1)} %get-tuple-element.4), channel_id=1, source_target_pairs={{1,0},{2,1},{3,2},{4,3},{5,4},{6,5},{7,6},{8,7},{9,8},{10,9},{11,1... | collective-permute-start | bytes 442376 | tf_op jit(solution)/shard_map/ppermute | solution.py:23
  65.3 7.5 copy-start.1
  65.4 284.0 %all-gather.3.cloned.1.call-start = ((), (), s32[]{:S(2)}) async-start(), calls=%async_computation.2 | async-start | bytes 5013504 | tf_op jit(solution)/shard_map/all_gather | solution.py:58
  66.5 4.5 collective-permute-start.6
  68.4 10.4 %collective-permute-start.7 = (f32[96,3,128]{2,0,1:T(8,128)S(1)}, f32[96,3,128]{2,0,1:T(8,128)S(1)}, u32[]{:S(2)}, u32[]{:S(2)}) collective-permute-start(f32[96,3,128]{2,0,1:T(8,128)S(1)} %get-tuple-element.2), channel_id=1, source_target_pairs={{1,0},{2,1},{3,2},{4,3},{5,4},{6,5},{7,6},{8,7},{9,8},{10,9},{11,1... | collective-permute-start | bytes 442376 | tf_op jit(solution)/shard_map/ppermute | solution.py:23
  83.1 560.7 %reduce-scatter.11.cloned.1.call-start = ((), (), s32[]{:S(2)}) async-start(), calls=%async_computation.5 | async-start | bytes 798720
  211.5 716.9 %reduce-scatter.9.cloned.1.call-start = ((), (), s32[]{:S(2)}) async-start(), calls=%async_computation.4 | async-start | bytes 798720
Sparse Core Ops, SparseCore 0:
  65.5 138.8 all-gather.4
  208.7 140.5 all-gather.2
  353.3 290.4 reduce-scatter.10
  647.9 280.4 reduce-scatter.8
where the time goes:
time: 935 us
  waiting for transfers between devices  854 us (91%)
  matrix products  29.7 us (3%)
  starting transfers between devices  28.7 us (3%)
  between operations  14.1 us (2%)
    unnamed x6, waiting for transfers between devices  572 us
    all_gather x1, waiting for transfers between devices, per_device(): lax.all_gather(image, 'row', axis=0, tiled=True)  138 us
    all_gather x1, waiting for transfers between devices, per_device(): lax.all_gather(y_now, 'row', axis=0, tiled=True)  121 us
    ppermute x4, waiting for transfers between devices, with_halo(): lax.ppermute(lax.slice_in_dim(block, 0, width, axis=dim), axis, backward)  22 us
    ppermute x4, starting transfers between devices, with_halo(): lax.ppermute(lax.slice_in_dim(block, block.shape[dim] - width, None, axis...  19 us
  transfers between devices with their start and end apart: 12, of which 9 were waited for; matrix products, arithmetic and copies ran while one was open for 3% of the time, Pallas kernels for 0%

commit v1 on v0

v1 whole, which is shorter than its diff:
```python
import functools

import jax
import jax.numpy as jnp
from jax import lax
from jax.experimental import pallas as pl
from jax.experimental.pallas import tpu as pltpu
from jax.sharding import PartitionSpec as P

REACH = 3
DEGREE = 3

CENTER = 0.5
HALF_WIDTH = 1.5
HSCALE = 0.1

LANES = 128
OWN = 6
PAIRS = OWN // 2
WINDOW = 8
MESH = pl.DeviceIdType.MESH


def split_high_low(value):
    high = value.astype(jnp.bfloat16)
    low = (value - high.astype(jnp.float32)).astype(jnp.bfloat16)
    return high, low


def dot_last(left, right):
    return lax.dot_general(
        left, right, (((1,), (1,)), ((), ())), preferred_element_type=jnp.float32
    )


def kernel(
    ring,
    states,
    coupling,
    vectors,
    hblocks,
    out_gram,
    out_ham,
    raw,
    band_high,
    band_low,
    fields,
    halo,
    operand,
    acc,
    image,
    blocks,
    image_block,
    sibling,
    side_high,
    side_low,
    other,
    products,
    parts,
    sums,
    last,
    load_sem,
    halo_send,
    halo_recv,
    swap_send,
    swap_recv,
    sib_send,
    sib_recv,
    ring_send,
    ring_recv,
    first_send,
    first_recv,
    second_send,
    second_recv,
):
    quarter = ring // 2
    half = ring // 2
    line = ring
    rows = states // quarter

    row = lax.axis_index("row")
    col = lax.axis_index("col")
    z, y_hi = row // 2, row % 2
    x = col // (2 * quarter)
    y_lo = (col // 2) % quarter
    core = col % 2
    y = y_hi * quarter + y_lo
    last_col = ring * 2 * quarter - 1

    def device(z_at, y_at, x_at, core_at):
        return (
            z_at * 2 + y_at // quarter,
            x_at * (2 * quarter) + (y_at % quarter) * 2 + core_at,
        )

    has_low, has_high = col > 0, col < last_col
    stays = y_hi == core
    moves = y_hi != core
    my_pos = jnp.where(core == 0, y, x)
    my_other = jnp.where(core == 0, x, y)
    my_half = my_pos // quarter
    my_piece = core * quarter + my_pos % quarter
    my_out = 2 * y_lo + core
    sends_to_self = jnp.logical_and(my_piece == my_out, x % 2 == my_half)

    def line_device(pos):
        return device(z, jnp.where(core == 0, pos, y), jnp.where(core == 0, x, pos), core)

    def owner_device(target, side):
        return device(z, side * quarter + my_piece // 2, target, my_piece % 2)

    src_core = my_out // quarter
    src_pos = (my_out % quarter + quarter * x) % line

    def source_device(at):
        return device(
            z, jnp.where(src_core == 0, src_pos, at), jnp.where(src_core == 0, at, src_pos), src_core
        )

    low_device, high_device = (row, col - 1), (row, col + 1)
    swap_device = device(z, core * quarter + y_lo, x, y_hi)
    sib_device = device(z, y, x, 1 - core)
    down_device = device((z + ring - 1) % ring, y, x, core)
    up_device = device((z + 1) % ring, y, x, core)

    load = pltpu.make_async_copy(hblocks, raw, load_sem.at[0])
    load.start()

    barrier = pltpu.get_barrier_semaphore()

    def greet(target, when=None):
        def signal():
            pl.semaphore_signal(barrier, inc=1, device_id=target, device_id_type=MESH)

        if when is None:
            signal()
        else:
            pl.when(when)(signal)

    greet(low_device, has_low)
    greet(high_device, has_high)
    greet(swap_device, moves)
    greet(sib_device)
    greet(down_device)
    greet(up_device)
    for pos in range(line):
        greet(line_device(pos), my_pos != pos)
    for item in range(half):
        target = 2 * item + my_half
        for side in range(2):
            is_self = sends_to_self & (target == x) & (side == y_hi)
            greet(owner_device(target, side), jnp.logical_not(is_self))
    for at in range(line):
        is_self = sends_to_self & (my_other == at)
        greet(source_device(at), jnp.logical_not(is_self))

    for a in range(OWN):
        fields[0, a] = vectors[:, a, :]

    greetings = (
        has_low.astype(jnp.int32)
        + has_high.astype(jnp.int32)
        + moves.astype(jnp.int32)
        + 3
        + (line - 1)
        + 2 * half
        + line
        - 2 * sends_to_self.astype(jnp.int32)
    )
    pl.semaphore_wait(barrier, greetings)

    unfinished = []

    def remote(src, dst, send, recv, target):
        return pltpu.make_async_remote_copy(
            src_ref=src,
            dst_ref=dst,
            send_sem=send,
            recv_sem=recv,
            device_id=target,
            device_id_type=MESH,
        )

    def start(copy, when=None):
        if when is None:
            copy.start()
            unfinished.append(copy.wait_send)
        else:
            pl.when(when)(copy.start)
            unfinished.append(lambda: pl.when(when)(copy.wait_send))

    def halo_copy(step, side):
        if side == 0:
            src, target = fields.at[step, pl.ds(OWN - REACH, REACH)], high_device
        else:
            src, target = fields.at[step, pl.ds(0, REACH)], low_device
        return remote(
            src, halo.at[step, side], halo_send.at[step, side], halo_recv.at[step, side], target
        )

    def send_halo(step):
        start(halo_copy(step, 0), has_high)
        start(halo_copy(step, 1), has_low)

    send_halo(0)

    load.wait()
    zero_block = jnp.zeros((LANES, LANES), jnp.bfloat16)
    for p in range(PAIRS):
        for band in (band_high, band_low):
            band[p, pl.ds(0, LANES), pl.ds((WINDOW - 1) * LANES, LANES)] = zero_block
            band[p, pl.ds(LANES, LANES), pl.ds(0, LANES)] = zero_block
        for second in range(2):
            a = 2 * p + second
            for o in range(2 * REACH + 1):
                scaled = HSCALE * raw[a, o]
                if o != REACH:
                    bond = coupling[a, o if o < REACH else o - 1]
                    scaled = scaled * bond.astype(jnp.float32)
                high, low = split_high_low(scaled)
                at = (pl.ds(second * LANES, LANES), pl.ds((o + second) * LANES, LANES))
                band_high[(p,) + at] = high
                band_low[(p,) + at] = low

    def put_operand(where, value):
        high, low = split_high_low(value)
        operand[pl.ds(0, states), pl.ds(where * LANES, LANES)] = high
        operand[pl.ds(states, states), pl.ds(where * LANES, LANES)] = low

    def band_product(p, begin, end):
        both = dot_last(
            operand[:, begin * LANES : end * LANES],
            band_high[p, :, (begin - 2 * p) * LANES : (end - 2 * p) * LANES],
        )
        rest = dot_last(
            operand[:states, begin * LANES : end * LANES],
            band_low[p, :, (begin - 2 * p) * LANES : (end - 2 * p) * LANES],
        )
        return both[:states] + both[states:] + rest

    def clear_edge(begin):
        operand[:, pl.ds(begin * LANES, REACH * LANES)] = jnp.zeros(
            (2 * states, REACH * LANES), jnp.bfloat16
        )

    pl.when(jnp.logical_not(has_low))(lambda: clear_edge(0))
    pl.when(jnp.logical_not(has_high))(lambda: clear_edge(REACH + OWN))

    def apply_own(step):
        for a in range(OWN):
            put_operand(REACH + a, fields[step, a])
        for p in range(PAIRS):
            begin, end = max(REACH, 2 * p), min(REACH + OWN, 2 * p + WINDOW)
            acc[p] = band_product(p, begin, end)

    def apply_halo(step):
        def take(side, begin):
            halo_copy(step, side).wait_recv()
            for a in range(REACH):
                put_operand(begin + a, halo[step, side, a])

        pl.when(has_low)(lambda: take(0, 0))
        for p in range(PAIRS):
            if 2 * p < REACH:
                acc[p] = acc[p] + band_product(p, 2 * p, REACH)
        pl.when(has_high)(lambda: take(1, REACH + OWN))
        for p in range(PAIRS):
            if 2 * p + WINDOW > REACH + OWN:
                acc[p] = acc[p] + band_product(p, REACH + OWN, 2 * p + WINDOW)

    def acted(a):
        return acc[a // 2, :, pl.ds((a % 2) * LANES, LANES)]

    for step in range(DEGREE):
        apply_own(step)
        apply_halo(step)
        for a in range(OWN):
            now = fields[step, a]
            if step == 0:
                fields[1, a] = (acted(a) - CENTER * now) / HALF_WIDTH
            else:
                fields[step + 1, a] = (
                    2.0 * (acted(a) - CENTER * now) / HALF_WIDTH - fields[step - 1, a]
                )
        send_halo(step + 1)

    def ring_copy(slot, chunk):
        part = pl.ds(chunk * REACH, REACH)
        upward = slot > half or (slot == half and chunk == 1)
        src, target = ((slot + 1) % ring, up_device) if upward else (slot - 1, down_device)
        return remote(
            blocks.at[src, part],
            blocks.at[slot, part],
            ring_send.at[slot, chunk],
            ring_recv.at[slot, chunk],
            target,
        )

    def ring_pieces(distance):
        if distance == half:
            return [(half, 0), (half, 1)]
        return [(slot, chunk) for chunk in range(2) for slot in (distance, ring - distance)]

    def swap_copy(at):
        src, dst = ((fields.at[DEGREE], blocks.at[0]), (image, image_block))[at]
        return remote(src, dst, swap_send.at[at], swap_recv.at[at], swap_device)

    def sib_copy(at):
        src = (blocks.at[0], image_block)[at]
        return remote(src, sibling.at[at], sib_send.at[at], sib_recv.at[at], sib_device)

    def keep_field():
        blocks[0] = fields[DEGREE]
        for piece in ring_pieces(1):
            ring_copy(*piece).start()

    def keep_image():
        image_block[...] = image[...]

    def take_field():
        swap_copy(0).wait_recv()
        for piece in ring_pieces(1):
            ring_copy(*piece).start()

    start(swap_copy(0), moves)
    pl.when(stays)(keep_field)
    for piece in ring_pieces(1):
        unfinished.append(ring_copy(*piece).wait_send)

    apply_own(DEGREE)
    apply_halo(DEGREE)
    for a in range(OWN):
        image[a] = acted(a)
    start(swap_copy(1), moves)
    pl.when(stays)(keep_image)
    pl.when(moves)(take_field)
    start(sib_copy(0))

    def forward(distance):
        for slot, chunk in ring_pieces(distance):
            ring_copy(slot, chunk).wait_recv()
            if distance < half:
                beyond = slot + 1 if slot < half else slot - 1
                if beyond != half or chunk == (0 if slot < half else 1):
                    start(ring_copy(beyond, chunk))

    def put_side(begin, source):
        for a in range(OWN):
            high, low = split_high_low(source(a))
            at = (pl.ds(begin, states), pl.ds(a * LANES, LANES))
            side_high[at] = high
            side_low[at] = low

    own_rows = pl.multiple_of(core * (2 * states), 2 * states)
    sib_rows = pl.multiple_of((1 - core) * (2 * states), 2 * states)
    put_side(own_rows, lambda a: blocks[0, a])

    forward(1)

    pl.when(moves)(swap_copy(1).wait_recv)
    start(sib_copy(1))
    put_side(own_rows + states, lambda a: image_block[a])
    sib_copy(0).wait_recv()
    put_side(sib_rows, lambda a: sibling[0, a])
    sib_copy(1).wait_recv()
    put_side(sib_rows + states, lambda a: sibling[1, a])

    def first_copy(slot, piece):
        target = (z + slot) % ring
        pos = (piece + quarter * target) % line
        copy = remote(
            products.at[slot, pl.ds(piece * rows, rows)],
            parts.at[target // 2, my_pos],
            first_send.at[slot, piece],
            first_recv.at[target // 2, my_pos],
            line_device(pos),
        )
        return copy, pos, target // 2

    def multiply(slot):
        for a in range(OWN):
            high, low = split_high_low(blocks[slot, a])
            other[pl.ds(0, states), pl.ds(a * LANES, LANES)] = high
            other[pl.ds(states, states), pl.ds(a * LANES, LANES)] = low
        both = dot_last(other[...], side_high[...])
        rest = dot_last(other[:states], side_low[...])
        products[slot] = both[:states] + both[states:] + rest
        for piece in range(quarter):
            copy, pos, item = first_copy(slot, piece)

            def keep(item=item, piece=piece):
                parts[item, my_pos] = products[slot, pl.ds(piece * rows, rows), :]

            start(copy, pos != my_pos)
            pl.when(pos == my_pos)(keep)

    multiply(0)
    for distance in range(1, half + 1):
        if distance > 1:
            forward(distance)
        multiply(distance)
        if distance != half:
            multiply(ring - distance)

    order = sorted(range(ring), key=lambda d: (min(d, ring - d), d))
    even = [d for d in order if d % 2 == 0]
    odd = [d for d in order if d % 2 == 1]
    parity = (z + my_half) % 2
    spans = []
    for side in range(2):
        begin = side * 2 * states // LANES * LANES
        end = -(-(side + 1) * 2 * states // LANES) * LANES
        spans.append((begin, end))

    def second_copy(item, side, target):
        begin, end = spans[side]
        return remote(
            sums.at[item, :, pl.ds(begin, end - begin)],
            last.at[my_other],
            second_send.at[item, side],
            second_recv.at[my_other],
            owner_device(target, side),
        )

    for at in range(half):
        slot = jnp.where(parity == 0, even[at], odd[at])
        target = (z + slot) % ring
        item = target // 2
        for pos in range(line):
            arrival = remote(
                parts.at[item, pos],
                parts.at[item, pos],
                first_send.at[0, 0],
                first_recv.at[item, pos],
                line_device(pos),
            )
            pl.when(my_pos != pos)(arrival.wait_recv)
        total = parts[item, 0]
        for pos in range(1, line):
            total = total + parts[item, pos]
        sums[item] = total
        for side in range(2):
            begin, end = spans[side]
            is_self = sends_to_self & (target == x) & (side == y_hi)

            def keep_sum(item=item, begin=begin, end=end):
                last[my_other] = sums[item, :, pl.ds(begin, end - begin)]

            start(second_copy(item, side, target), jnp.logical_not(is_self))
            pl.when(is_self)(keep_sum)

    for at in range(line):
        is_self = sends_to_self & (my_other == at)
        arrival = remote(
            last.at[at], last.at[at], second_send.at[0, 0], second_recv.at[at], source_device(at)
        )
        pl.when(jnp.logical_not(is_self))(arrival.wait_recv)
    total = last[0]
    for at in range(1, line):
        total = total + last[at]
    skip = 2 * states - spans[1][0]
    gram = jnp.where(y_hi == 0, total[:, :states], total[:, skip : skip + states])
    ham = jnp.where(
        y_hi == 0, total[:, states : 2 * states], total[:, skip + states : skip + 2 * states]
    )
    out_gram[...] = gram
    out_ham[...] = ham

    for finish in unfinished:
        finish()


def per_device(ring, vectors, hblocks, coupling):
    states = vectors.shape[0]
    quarter, half, line = ring // 2, ring // 2, ring
    rows = states // quarter
    width = -(-2 * states // LANES) * LANES
    f32, bf16 = jnp.float32, jnp.bfloat16
    dma = pltpu.SemaphoreType.DMA
    gram, ham = pl.pallas_call(
        functools.partial(kernel, ring, states),
        out_shape=[jax.ShapeDtypeStruct((rows, states), f32)] * 2,
        in_specs=[
            pl.BlockSpec(memory_space=pltpu.SMEM),
            pl.BlockSpec(memory_space=pltpu.VMEM),
            pl.BlockSpec(memory_space=pl.ANY),
        ],
        out_specs=[pl.BlockSpec(memory_space=pltpu.VMEM)] * 2,
        scratch_shapes=[
            pltpu.VMEM((OWN, 2 * REACH + 1, LANES, LANES), f32),
            pltpu.VMEM((PAIRS, 2 * LANES, WINDOW * LANES), bf16),
            pltpu.VMEM((PAIRS, 2 * LANES, WINDOW * LANES), bf16),
            pltpu.VMEM((DEGREE + 1, OWN, states, LANES), f32),
            pltpu.VMEM((DEGREE + 1, 2, REACH, states, LANES), f32),
            pltpu.VMEM((2 * states, (OWN + 2 * REACH) * LANES), bf16),
            pltpu.VMEM((PAIRS, states, 2 * LANES), f32),
            pltpu.VMEM((OWN, states, LANES), f32),
            pltpu.VMEM((ring, OWN, states, LANES), f32),
            pltpu.VMEM((OWN, states, LANES), f32),
            pltpu.VMEM((2, OWN, states, LANES), f32),
            pltpu.VMEM((4 * states, OWN * LANES), bf16),
            pltpu.VMEM((4 * states, OWN * LANES), bf16),
            pltpu.VMEM((2 * states, OWN * LANES), bf16),
            pltpu.VMEM((ring, states, 4 * states), f32),
            pltpu.VMEM((half, line, rows, 4 * states), f32),
            pltpu.VMEM((half, rows, 4 * states), f32),
            pltpu.VMEM((line, rows, width), f32),
            dma((1,)),
            dma((DEGREE + 1, 2)),
            dma((DEGREE + 1, 2)),
            dma((2,)),
            dma((2,)),
            dma((2,)),
            dma((2,)),
            dma((ring, 2)),
            dma((ring, 2)),
            dma((ring, quarter)),
            dma((half, line)),
            dma((half, 2)),
            dma((line,)),
        ],
        compiler_params=pltpu.CompilerParams(
            collective_id=0, has_side_effects=True, vmem_limit_bytes=48 * 1024 * 1024
        ),
    )(coupling, vectors, hblocks)
    return ham.T, gram.T


def solution(mesh):
    in_specs = (P("row", "col", None), P("col", None, None, None), P("col", None))
    out_specs = (P("row", "col"), P("row", "col"))
    ring = mesh.shape["row"] // 2
    return jax.shard_map(
        functools.partial(per_device, ring),
        mesh=mesh,
        in_specs=in_specs,
        out_specs=out_specs,
        check_vma=False,
    )
```

time: 935 us -> 103 us (0.11)
  the two profiles are of different devices: /device:TPU:119 before, /device:TPU:24 now
where the time goes in v1:
time: 103 us
  Pallas kernels  97.2 us (94%)
  local copies, waits for them, and re-layouts  4.8 us (5%)
    pallas_call x1, Pallas kernels, per_device(): pl.pallas_call(functools.partial(kernel, ring, states), out_shape=[jax.Sh...  97.2 us
    unnamed x7, local copies, waits for them, and re-layouts  4.8 us

profile of v1, /device:TPU:24, one launch (start us, length us, event | category | flops | bytes accessed | tf_op | source)
XLA Modules:
  0.0 102.7 jit_solution(11092330630035779068)
XLA Ops:
  0.6 1.1 %copy.5.vectors = f32[96,6,128]{2,1,0:T(8,128)S(1)} copy(f32[96,6,128]{2,0,1:T(8,128)} %param.3) | data formatting | bytes 589824 | tf_op args[0]
  1.8 0.0 copy-start
  1.8 1.8 %copy-done = f32[6,7,128,128]{3,2,1,0:T(8,128)S(1)} copy-done((f32[6,7,128,128]{3,2,1,0:T(8,128)S(1)}, f32[6,7,128,128]{3,2,1,0:T(8,128)}, u32[]{:S(2)}) %copy-start) | copy-done | bytes 2752536
  3.6 0.0 copy-start.1
  3.6 0.7 copy-done.1
  4.2 97.2 %shard_map.50 = (f32[24,96]{1,0:T(8,128)S(1)}, f32[24,96]{1,0:T(8,128)S(1)}) custom-call(s32[6,6]{1,0:T(8,128)S(1)} %copy-done.1, f32[96,6,128]{2,1,0:T(8,128)S(1)} %copy.5.vectors, f32[6,7,128,128]{3,2,1,0:T(8,128)S(1)} %copy-done), custom_call_target="tpu_custom_call" | custom-call | tf_op jit(solution)/shard_map/pallas_call | solution.py:480
  101.5 0.6 copy.8
  102.1 0.6 copy.9
Async XLA Ops:
  1.8 1.8 %copy-start = (f32[6,7,128,128]{3,2,1,0:T(8,128)S(1)}, f32[6,7,128,128]{3,2,1,0:T(8,128)}, u32[]{:S(2)}) copy-start(f32[6,7,128,128]{3,2,1,0:T(8,128)} %hblocks.1) | copy-start | bytes 8257540
  3.6 0.7 copy-start.1

commit v2 on v1

--- a/solution.py
+++ b/solution.py
@@ -18,6 +18,7 @@
 OWN = 6
 PAIRS = OWN // 2
 WINDOW = 8
+GROUPS = 2
 MESH = pl.DeviceIdType.MESH
 
 
@@ -41,6 +42,7 @@
     hblocks,
     out_gram,
     out_ham,
+    bonds,
     raw,
     band_high,
     band_low,
@@ -77,6 +79,7 @@
     half = ring // 2
     line = ring
     rows = states // quarter
+    part = states // GROUPS
 
     row = lax.axis_index("row")
     col = lax.axis_index("col")
@@ -124,6 +127,10 @@
     up_device = device((z + 1) % ring, y, x, core)
 
     load = pltpu.make_async_copy(hblocks, raw, load_sem.at[0])
+    load_field = pltpu.make_async_copy(vectors, fields.at[0], load_sem.at[1])
+    load_bonds = pltpu.make_async_copy(coupling, bonds, load_sem.at[2])
+    load_field.start()
+    load_bonds.start()
     load.start()
 
     barrier = pltpu.get_barrier_semaphore()
@@ -154,9 +161,6 @@
         is_self = sends_to_self & (my_other == at)
         greet(source_device(at), jnp.logical_not(is_self))
 
-    for a in range(OWN):
-        fields[0, a] = vectors[:, a, :]
-
     greetings = (
         has_low.astype(jnp.int32)
         + has_high.astype(jnp.int32)
@@ -167,6 +171,7 @@
         + line
         - 2 * sends_to_self.astype(jnp.int32)
     )
+    load_field.wait()
     pl.semaphore_wait(barrier, greetings)
 
     unfinished = []
@@ -189,21 +194,27 @@
             pl.when(when)(copy.start)
             unfinished.append(lambda: pl.when(when)(copy.wait_send))
 
-    def halo_copy(step, side):
-        if side == 0:
-            src, target = fields.at[step, pl.ds(OWN - REACH, REACH)], high_device
-        else:
-            src, target = fields.at[step, pl.ds(0, REACH)], low_device
+    def group_rows(g):
+        return pl.ds(g * part, part)
+
+    def halo_copy(step, side, g):
+        first, target = (OWN - REACH, high_device) if side == 0 else (0, low_device)
         return remote(
-            src, halo.at[step, side], halo_send.at[step, side], halo_recv.at[step, side], target
-        )
-
-    def send_halo(step):
-        start(halo_copy(step, 0), has_high)
-        start(halo_copy(step, 1), has_low)
-
-    send_halo(0)
-
+            fields.at[step, pl.ds(first, REACH), group_rows(g)],
+            halo.at[step, side, :, group_rows(g)],
+            halo_send.at[step, side, g],
+            halo_recv.at[step, side, g],
+            target,
+        )
+
+    def send_halo(step, g):
+        start(halo_copy(step, 0, g), has_high)
+        start(halo_copy(step, 1, g), has_low)
+
+    for g in range(GROUPS):
+        send_halo(0, g)
+
+    load_bonds.wait()
     load.wait()
     zero_block = jnp.zeros((LANES, LANES), jnp.bfloat16)
     for p in range(PAIRS):
@@ -215,28 +226,26 @@
             for o in range(2 * REACH + 1):
                 scaled = HSCALE * raw[a, o]
                 if o != REACH:
-                    bond = coupling[a, o if o < REACH else o - 1]
+                    bond = bonds[a, o if o < REACH else o - 1]
                     scaled = scaled * bond.astype(jnp.float32)
                 high, low = split_high_low(scaled)
                 at = (pl.ds(second * LANES, LANES), pl.ds((o + second) * LANES, LANES))
                 band_high[(p,) + at] = high
                 band_low[(p,) + at] = low
 
-    def put_operand(where, value):
+    def put_operand(g, where, value):
         high, low = split_high_low(value)
-        operand[pl.ds(0, states), pl.ds(where * LANES, LANES)] = high
-        operand[pl.ds(states, states), pl.ds(where * LANES, LANES)] = low
-
-    def band_product(p, begin, end):
+        operand[pl.ds(2 * g * part, part), pl.ds(where * LANES, LANES)] = high
+        operand[pl.ds((2 * g + 1) * part, part), pl.ds(where * LANES, LANES)] = low
+
+    def band_product(g, p, begin, end):
+        begin_row, columns = 2 * g * part, slice(begin * LANES, end * LANES)
+        window = slice((begin - 2 * p) * LANES, (end - 2 * p) * LANES)
         both = dot_last(
-            operand[:, begin * LANES : end * LANES],
-            band_high[p, :, (begin - 2 * p) * LANES : (end - 2 * p) * LANES],
-        )
-        rest = dot_last(
-            operand[:states, begin * LANES : end * LANES],
-            band_low[p, :, (begin - 2 * p) * LANES : (end - 2 * p) * LANES],
-        )
-        return both[:states] + both[states:] + rest
+            operand[begin_row : begin_row + 2 * part, columns], band_high[p, :, window]
+        )
+        rest = dot_last(operand[begin_row : begin_row + part, columns], band_low[p, :, window])
+        return both[:part] + both[part:] + rest
 
     def clear_edge(begin):
         operand[:, pl.ds(begin * LANES, REACH * LANES)] = jnp.zeros(
@@ -246,51 +255,38 @@
     pl.when(jnp.logical_not(has_low))(lambda: clear_edge(0))
     pl.when(jnp.logical_not(has_high))(lambda: clear_edge(REACH + OWN))
 
-    def apply_own(step):
+    def apply_own(step, g):
         for a in range(OWN):
-            put_operand(REACH + a, fields[step, a])
+            put_operand(g, REACH + a, fields[step, a, group_rows(g)])
         for p in range(PAIRS):
             begin, end = max(REACH, 2 * p), min(REACH + OWN, 2 * p + WINDOW)
-            acc[p] = band_product(p, begin, end)
-
-    def apply_halo(step):
+            acc[p, group_rows(g)] = band_product(g, p, begin, end)
+
+    def apply_halo(step, g):
         def take(side, begin):
-            halo_copy(step, side).wait_recv()
+            halo_copy(step, side, g).wait_recv()
             for a in range(REACH):
-                put_operand(begin + a, halo[step, side, a])
+                put_operand(g, begin + a, halo[step, side, a, group_rows(g)])
 
         pl.when(has_low)(lambda: take(0, 0))
-        for p in range(PAIRS):
-            if 2 * p < REACH:
-                acc[p] = acc[p] + band_product(p, 2 * p, REACH)
         pl.when(has_high)(lambda: take(1, REACH + OWN))
         for p in range(PAIRS):
+            total = acc[p, group_rows(g)]
+            if 2 * p < REACH:
+                total = total + band_product(g, p, 2 * p, REACH)
             if 2 * p + WINDOW > REACH + OWN:
-                acc[p] = acc[p] + band_product(p, REACH + OWN, 2 * p + WINDOW)
-
-    def acted(a):
-        return acc[a // 2, :, pl.ds((a % 2) * LANES, LANES)]
-
-    for step in range(DEGREE):
-        apply_own(step)
-        apply_halo(step)
-        for a in range(OWN):
-            now = fields[step, a]
-            if step == 0:
-                fields[1, a] = (acted(a) - CENTER * now) / HALF_WIDTH
-            else:
-                fields[step + 1, a] = (
-                    2.0 * (acted(a) - CENTER * now) / HALF_WIDTH - fields[step - 1, a]
-                )
-        send_halo(step + 1)
+                total = total + band_product(g, p, REACH + OWN, 2 * p + WINDOW)
+            acc[p, group_rows(g)] = total
+
+    def acted(g, a):
+        return acc[a // 2, group_rows(g), pl.ds((a % 2) * LANES, LANES)]
 
     def ring_copy(slot, chunk):
-        part = pl.ds(chunk * REACH, REACH)
         upward = slot > half or (slot == half and chunk == 1)
         src, target = ((slot + 1) % ring, up_device) if upward else (slot - 1, down_device)
         return remote(
-            blocks.at[src, part],
-            blocks.at[slot, part],
+            blocks.at[src, :, group_rows(chunk)],
+            blocks.at[slot, :, group_rows(chunk)],
             ring_send.at[slot, chunk],
             ring_recv.at[slot, chunk],
             target,
@@ -301,40 +297,25 @@
             return [(half, 0), (half, 1)]
         return [(slot, chunk) for chunk in range(2) for slot in (distance, ring - distance)]
 
-    def swap_copy(at):
+    def swap_copy(at, g):
         src, dst = ((fields.at[DEGREE], blocks.at[0]), (image, image_block))[at]
-        return remote(src, dst, swap_send.at[at], swap_recv.at[at], swap_device)
-
-    def sib_copy(at):
+        return remote(
+            src.at[:, group_rows(g)],
+            dst.at[:, group_rows(g)],
+            swap_send.at[at, g],
+            swap_recv.at[at, g],
+            swap_device,
+        )
+
+    def sib_copy(at, g):
         src = (blocks.at[0], image_block)[at]
-        return remote(src, sibling.at[at], sib_send.at[at], sib_recv.at[at], sib_device)
-
-    def keep_field():
-        blocks[0] = fields[DEGREE]
-        for piece in ring_pieces(1):
-            ring_copy(*piece).start()
-
-    def keep_image():
-        image_block[...] = image[...]
-
-    def take_field():
-        swap_copy(0).wait_recv()
-        for piece in ring_pieces(1):
-            ring_copy(*piece).start()
-
-    start(swap_copy(0), moves)
-    pl.when(stays)(keep_field)
-    for piece in ring_pieces(1):
-        unfinished.append(ring_copy(*piece).wait_send)
-
-    apply_own(DEGREE)
-    apply_halo(DEGREE)
-    for a in range(OWN):
-        image[a] = acted(a)
-    start(swap_copy(1), moves)
-    pl.when(stays)(keep_image)
-    pl.when(moves)(take_field)
-    start(sib_copy(0))
+        return remote(
+            src.at[:, group_rows(g)],
+            sibling.at[at, :, group_rows(g)],
+            sib_send.at[at, g],
+            sib_recv.at[at, g],
+            sib_device,
+        )
 
     def forward(distance):
         for slot, chunk in ring_pieces(distance):
@@ -342,7 +323,38 @@
             if distance < half:
                 beyond = slot + 1 if slot < half else slot - 1
                 if beyond != half or chunk == (0 if slot < half else 1):
-                    start(ring_copy(beyond, chunk))
+                    ring_copy(beyond, chunk).start()
+
+    def begin_ring(g):
+        for slot, chunk in ring_pieces(1):
+            if chunk == g:
+                ring_copy(slot, chunk).start()
+        sib_copy(0, g).start()
+
+    for distance in range(1, half + 1):
+        for piece in ring_pieces(distance):
+            unfinished.append(ring_copy(*piece).wait_send)
+    for at in range(2):
+        for g in range(GROUPS):
+            unfinished.append(sib_copy(at, g).wait_send)
+
+    def keep_field(g):
+        blocks[0, :, group_rows(g)] = fields[DEGREE, :, group_rows(g)]
+        begin_ring(g)
+
+    def take_field():
+        for g in range(GROUPS):
+            swap_copy(0, g).wait_recv()
+            begin_ring(g)
+
+    def keep_image(g):
+        image_block[:, group_rows(g)] = image[:, group_rows(g)]
+        sib_copy(1, g).start()
+
+    def take_image():
+        for g in range(GROUPS):
+            swap_copy(1, g).wait_recv()
+            sib_copy(1, g).start()
 
     def put_side(begin, source):
         for a in range(OWN):
@@ -353,16 +365,47 @@
 
     own_rows = pl.multiple_of(core * (2 * states), 2 * states)
     sib_rows = pl.multiple_of((1 - core) * (2 * states), 2 * states)
+
+    for step in range(DEGREE):
+        for g in range(GROUPS):
+            apply_own(step, g)
+            apply_halo(step, g)
+            for a in range(OWN):
+                now = fields[step, a, group_rows(g)]
+                if step == 0:
+                    later = (acted(g, a) - CENTER * now) / HALF_WIDTH
+                else:
+                    before = fields[step - 1, a, group_rows(g)]
+                    later = 2.0 * (acted(g, a) - CENTER * now) / HALF_WIDTH - before
+                fields[step + 1, a, group_rows(g)] = later
+            send_halo(step + 1, g)
+            if step == DEGREE - 1:
+                start(swap_copy(0, g), moves)
+                pl.when(stays)(functools.partial(keep_field, g))
+
+    for g in range(GROUPS):
+        apply_own(DEGREE, g)
+        apply_halo(DEGREE, g)
+        for a in range(OWN):
+            image[a, group_rows(g)] = acted(g, a)
+        start(swap_copy(1, g), moves)
+        pl.when(stays)(functools.partial(keep_image, g))
+        if g == 0:
+            pl.when(stays)(lambda: forward(1))
+    pl.when(moves)(take_field)
+    if half > 1:
+        pl.when(stays)(lambda: forward(2))
     put_side(own_rows, lambda a: blocks[0, a])
-
-    forward(1)
-
-    pl.when(moves)(swap_copy(1).wait_recv)
-    start(sib_copy(1))
+    for g in range(GROUPS):
+        sib_copy(0, g).wait_recv()
+    put_side(sib_rows, lambda a: sibling[0, a])
+    pl.when(moves)(lambda: forward(1))
+    pl.when(moves)(take_image)
+    for distance in range(3, half + 1):
+        pl.when(stays)(functools.partial(forward, distance))
     put_side(own_rows + states, lambda a: image_block[a])
-    sib_copy(0).wait_recv()
-    put_side(sib_rows, lambda a: sibling[0, a])
-    sib_copy(1).wait_recv()
+    for g in range(GROUPS):
+        sib_copy(1, g).wait_recv()
     put_side(sib_rows + states, lambda a: sibling[1, a])
 
     def first_copy(slot, piece):
@@ -397,7 +440,7 @@
     multiply(0)
     for distance in range(1, half + 1):
         if distance > 1:
-            forward(distance)
+            pl.when(moves)(functools.partial(forward, distance))
         multiply(distance)
         if distance != half:
             multiply(ring - distance)
@@ -481,12 +524,13 @@
         functools.partial(kernel, ring, states),
         out_shape=[jax.ShapeDtypeStruct((rows, states), f32)] * 2,
         in_specs=[
-            pl.BlockSpec(memory_space=pltpu.SMEM),
-            pl.BlockSpec(memory_space=pltpu.VMEM),
+            pl.BlockSpec(memory_space=pl.ANY),
+            pl.BlockSpec(memory_space=pl.ANY),
             pl.BlockSpec(memory_space=pl.ANY),
         ],
         out_specs=[pl.BlockSpec(memory_space=pltpu.VMEM)] * 2,
         scratch_shapes=[
+            pltpu.SMEM((OWN, 2 * REACH), jnp.int32),
             pltpu.VMEM((OWN, 2 * REACH + 1, LANES, LANES), f32),
             pltpu.VMEM((PAIRS, 2 * LANES, WINDOW * LANES), bf16),
             pltpu.VMEM((PAIRS, 2 * LANES, WINDOW * LANES), bf16),
@@ -505,13 +549,13 @@
             pltpu.VMEM((half, line, rows, 4 * states), f32),
             pltpu.VMEM((half, rows, 4 * states), f32),
             pltpu.VMEM((line, rows, width), f32),
-            dma((1,)),
-            dma((DEGREE + 1, 2)),
-            dma((DEGREE + 1, 2)),
-            dma((2,)),
-            dma((2,)),
-            dma((2,)),
-            dma((2,)),
+            dma((3,)),
+            dma((DEGREE + 1, 2, GROUPS)),
+            dma((DEGREE + 1, 2, GROUPS)),
+            dma((2, GROUPS)),
+            dma((2, GROUPS)),
+            dma((2, GROUPS)),
+            dma((2, GROUPS)),
             dma((ring, 2)),
             dma((ring, 2)),
             dma((ring, quarter)),
@@ -520,9 +564,9 @@
             dma((line,)),
         ],
         compiler_params=pltpu.CompilerParams(
-            collective_id=0, has_side_effects=True, vmem_limit_bytes=48 * 1024 * 1024
+            collective_id=0, has_side_effects=True, vmem_limit_bytes=60 * 1024 * 1024
         ),
-    )(coupling, vectors, hblocks)
+    )(coupling, jnp.swapaxes(vectors, 0, 1), hblocks)
     return ham.T, gram.T
 
 

time: 103 us -> 97.3 us (0.945)
  the two profiles are of different devices: /device:TPU:24 before, /device:TPU:26 now
where the time goes in v2:
time: 97.3 us; the launch traced here: 97 us
  Pallas kernels  93.7 us (96%)
  local copies, waits for them, and re-layouts  2.61 us (3%)
    pallas_call x1, Pallas kernels, per_device(): pl.pallas_call(functools.partial(kernel, ring, states), out_shape=[jax.Sh...  93.7 us
    unnamed x2, local copies, waits for them, and re-layouts  2.61 us

profile of v2, /device:TPU:26, one launch (start us, length us, event | category | flops | bytes accessed | tf_op | source)
XLA Modules:
  0.0 97.0 jit_solution(6432144292605063566)
XLA Ops:
  0.6 93.7 %shard_map.50 = (f32[24,96]{1,0:T(8,128)}, f32[24,96]{1,0:T(8,128)}) custom-call(s32[6,6]{1,0:T(8,128)} %coupling.1, f32[6,96,128]{2,1,0:T(8,128)} %bitcast.3, f32[6,7,128,128]{3,2,1,0:T(8,128)} %hblocks.1), custom_call_target="tpu_custom_call" | custom-call | tf_op jit(solution)/shard_map/pallas_call | solution.py:523
  94.4 1.3 %copy.7 = f32[96,24]{0,1:T(8,128)} copy(f32[96,24]{0,1:T(8,128)} %bitcast.5) | data formatting | bytes 18432
  95.7 1.3 %copy.8 = f32[96,24]{0,1:T(8,128)} copy(f32[96,24]{0,1:T(8,128)} %bitcast.4) | data formatting | bytes 18432

commit v3 on v2

--- a/solution.py
+++ b/solution.py
@@ -40,8 +40,7 @@
     coupling,
     vectors,
     hblocks,
-    out_gram,
-    out_ham,
+    out,
     bonds,
     raw,
     band_high,
@@ -399,7 +398,6 @@
     for g in range(GROUPS):
         sib_copy(0, g).wait_recv()
     put_side(sib_rows, lambda a: sibling[0, a])
-    pl.when(moves)(lambda: forward(1))
     pl.when(moves)(take_image)
     for distance in range(3, half + 1):
         pl.when(stays)(functools.partial(forward, distance))
@@ -438,6 +436,7 @@
             pl.when(pos == my_pos)(keep)
 
     multiply(0)
+    pl.when(moves)(lambda: forward(1))
     for distance in range(1, half + 1):
         if distance > 1:
             pl.when(moves)(functools.partial(forward, distance))
@@ -506,8 +505,8 @@
     ham = jnp.where(
         y_hi == 0, total[:, states : 2 * states], total[:, skip + states : skip + 2 * states]
     )
-    out_gram[...] = gram
-    out_ham[...] = ham
+    out[0] = ham
+    out[1] = gram
 
     for finish in unfinished:
         finish()
@@ -520,15 +519,15 @@
     width = -(-2 * states // LANES) * LANES
     f32, bf16 = jnp.float32, jnp.bfloat16
     dma = pltpu.SemaphoreType.DMA
-    gram, ham = pl.pallas_call(
+    both = pl.pallas_call(
         functools.partial(kernel, ring, states),
-        out_shape=[jax.ShapeDtypeStruct((rows, states), f32)] * 2,
+        out_shape=jax.ShapeDtypeStruct((2, rows, states), f32),
         in_specs=[
             pl.BlockSpec(memory_space=pl.ANY),
             pl.BlockSpec(memory_space=pl.ANY),
             pl.BlockSpec(memory_space=pl.ANY),
         ],
-        out_specs=[pl.BlockSpec(memory_space=pltpu.VMEM)] * 2,
+        out_specs=pl.BlockSpec(memory_space=pltpu.VMEM),
         scratch_shapes=[
             pltpu.SMEM((OWN, 2 * REACH), jnp.int32),
             pltpu.VMEM((OWN, 2 * REACH + 1, LANES, LANES), f32),
@@ -567,7 +566,7 @@
             collective_id=0, has_side_effects=True, vmem_limit_bytes=60 * 1024 * 1024
         ),
     )(coupling, jnp.swapaxes(vectors, 0, 1), hblocks)
-    return ham.T, gram.T
+    return both[0].T, both[1].T
 
 
 def solution(mesh):

time: 97.3 us -> 94.4 us (0.970)
  the two profiles are of different devices: /device:TPU:26 before, /device:TPU:10 now
where the time goes in v3:
time: 94.4 us; the launch traced here: 94.2 us
  Pallas kernels  92.2 us (98%)
  local copies, waits for them, and re-layouts  1.33 us (1%)
    pallas_call x1, Pallas kernels, per_device(): pl.pallas_call(functools.partial(kernel, ring, states), out_shape=jax.Sha...  92.2 us

profile of v3, /device:TPU:10, one launch (start us, length us, event | category | flops | bytes accessed | tf_op | source)
XLA Modules:
  0.0 94.2 jit_solution(14898225644782312747)
XLA Ops:
  0.6 92.2 %shard_map.50 = f32[2,24,96]{2,1,0:T(8,128)} custom-call(s32[6,6]{1,0:T(8,128)} %coupling.1, f32[6,96,128]{2,1,0:T(8,128)} %bitcast.9, f32[6,7,128,128]{3,2,1,0:T(8,128)} %hblocks.1), custom_call_target="tpu_custom_call" | custom-call | tf_op jit(solution)/shard_map/pallas_call | solution.py:522
  92.9 1.3 %slice_bitcast_fusion = (f32[96,24]{0,1:T(8,128)}, f32[96,24]{0,1:T(8,128)}) fusion(f32[2,24,96]{2,1,0:T(8,128)} %shard_map.50), kind=kLoop, calls=%fused_computation | loop fusion | bytes 36864 | tf_op jit(solution)/shard_map/transpose | solution.py:569
